TPU v7x, 32 devices: a whole 2x2x4 slice. The times are simulated.
32 devices in a mesh: dp: 8 (over y, x, core), fsdp: 4 (over z).
Axes of the slice: x: 2, y: 2, z: 4, core: 2. Of those that a mesh axis runs over, the one named last changes fastest.
Arguments:
- source: bfloat16 [32768, 512], P(('dp', 'fsdp')), may hold values from -6 to 6
- target: bfloat16 [32768, 512], P(('dp', 'fsdp')), may hold values from -6 to 6
- source_segments: int32 [64, 512], P(('dp', 'fsdp')), may hold values from 0 to 7, never falling along the last dimension, each value on 1 to 256 neighbouring positions
- target_segments: int32 [64, 512], P(('dp', 'fsdp')), may hold values from 0 to 7, never falling along the last dimension, each value on 1 to 256 neighbouring positions
- target_language: int32 [64, 8], P(('dp', 'fsdp')), may hold values from 0 to 7
- cotangent: bfloat16 [32768, 512], P(('dp', 'fsdp')), may hold values from -6 to 6
- enc_qkv: bfloat16 [512, 1536], P(('dp', 'fsdp')), may hold values from -0.25 to 0.25
- enc_out: bfloat16 [512, 512], P(('dp', 'fsdp')), may hold values from -0.5 to 0.5
- enc_up: bfloat16 [512, 2048], P(('dp', 'fsdp')), may hold values from -0.25 to 0.25
- enc_down: bfloat16 [2048, 512], P(('dp', 'fsdp')), may hold values from -0.125 to 0.125
- enc_vecs: bfloat16 [512, 8], P(('dp', 'fsdp')), may hold values from -1.2 to 1.45, as said below
- enc_bias_up: bfloat16 [2048], P(('dp', 'fsdp')), may hold values from -2 to 2
- dec_qkv: bfloat16 [512, 1536], P(('dp', 'fsdp')), may hold values from -0.25 to 0.25
- dec_out: bfloat16 [512, 512], P(('dp', 'fsdp')), may hold values from -0.5 to 0.5
- cross_q: bfloat16 [512, 512], P(('dp', 'fsdp')), may hold values from -0.25 to 0.25
- cross_kv: bfloat16 [512, 1024], P(('dp', 'fsdp')), may hold values from -0.25 to 0.25
- cross_out: bfloat16 [512, 512], P(('dp', 'fsdp')), may hold values from -0.5 to 0.5
- dec_up: bfloat16 [512, 2048], P(('dp', 'fsdp')), may hold values from -0.25 to 0.25
- dec_down: bfloat16 [2048, 512], P(('dp', 'fsdp')), may hold values from -0.125 to 0.125
- dec_vecs: bfloat16 [512, 13], P(('dp', 'fsdp')), may hold values from -1.2 to 1.45, as said below
- dec_bias_up: bfloat16 [2048], P(('dp', 'fsdp')), may hold values from -2 to 2
- lang_table: bfloat16 [512, 8], P(('dp', 'fsdp')), may hold values from -4 to 4
Outputs:
- dec_output: bfloat16 [32768, 512], P(('dp', 'fsdp'))
- source_grad: bfloat16 [32768, 512], P(('dp', 'fsdp'))
- target_grad: bfloat16 [32768, 512], P(('dp', 'fsdp'))
- enc_qkv_grad: float32 [512, 1536], P(('dp', 'fsdp'))
- enc_out_grad: float32 [512, 512], P(('dp', 'fsdp'))
- enc_up_grad: float32 [512, 2048], P(('dp', 'fsdp'))
- enc_down_grad: float32 [2048, 512], P(('dp', 'fsdp'))
- enc_vecs_grad: float32 [512, 8], P(('dp', 'fsdp'))
- enc_bias_up_grad: float32 [2048], P(('dp', 'fsdp'))
- dec_qkv_grad: float32 [512, 1536], P(('dp', 'fsdp'))
- dec_out_grad: float32 [512, 512], P(('dp', 'fsdp'))
- cross_q_grad: float32 [512, 512], P(('dp', 'fsdp'))
- cross_kv_grad: float32 [512, 1024], P(('dp', 'fsdp'))
- cross_out_grad: float32 [512, 512], P(('dp', 'fsdp'))
- dec_up_grad: float32 [512, 2048], P(('dp', 'fsdp'))
- dec_down_grad: float32 [2048, 512], P(('dp', 'fsdp'))
- dec_vecs_grad: float32 [512, 13], P(('dp', 'fsdp'))
- dec_bias_up_grad: float32 [2048], P(('dp', 'fsdp'))
- lang_table_grad: float32 [512, 8], P(('dp', 'fsdp'))
Inputs may be any that keep to these rules, and one draw needn't show every extreme that they name: `source_segments`: within each row the numbers never fall; each of the 8 sentences holds 1 to 256 positions, and one holds exactly 256. `target_segments`: within each row the numbers never fall; each of the 8 sentences holds 1 to 256 positions, and one holds exactly 256. `enc_vecs`: columns 3 and 6 are gains, the others biases. `dec_vecs`: columns 3, 8 and 11 are gains, the others biases.
All inputs are finite; a program needn't handle non-finite values.
Results may differ from a plain program's by a relative error of at most 0.023.
Values may be sent and summed in bfloat16 or wider, within the bound.
No kernel may reach another device: no remote copies, remote signals or barrier semaphores. Data moves between devices by JAX's collectives and lax.ppermute only.
A program may use at most 256 MiB of HBM per device.

v0:
```python
import jax
import jax.numpy as jnp
from jax import lax
from jax.sharding import PartitionSpec as P

HDIM = 64
LANGS = 8


scale_dot = 0.125
norm_eps = 1e-05
masked_score = -1000000000.0
highest = lax.Precision.HIGHEST


def low_dot(left_operand, right_operand):
    return jnp.dot(left_operand, right_operand, preferred_element_type=jnp.float32)


def rows_inner(left_operand, right_operand):
    return lax.dot_general(
        left_operand, right_operand, (((0,), (0,)), ((), ())), preferred_element_type=jnp.float32
    )


def right_inner(left_operand, right_operand):
    return lax.dot_general(
        left_operand, right_operand, (((1,), (1,)), ((), ())), preferred_element_type=jnp.float32
    )


def column_sum(matrix_rows):
    return jnp.sum(matrix_rows, axis=0, dtype=jnp.float32)


def project(inputs_low, weight_part, bias_row):
    return (low_dot(inputs_low, weight_part) + bias_row).astype(jnp.bfloat16)


def smooth_gate(hidden):
    return jax.nn.gelu(hidden, approximate=True)


def norm_forward(summed, norm_gain, norm_shift):
    centred = summed - jnp.mean(summed, axis=-1, keepdims=True)
    inverse = lax.rsqrt(jnp.mean(centred * centred, axis=-1, keepdims=True) + norm_eps)
    normed = centred * inverse
    return (normed * norm_gain + norm_shift, (normed, inverse))


def norm_backward(grad_out, norm_gain, norm_saved):
    normed, inverse = norm_saved
    grad_gain = jnp.sum(grad_out * normed, axis=0)
    grad_shift = jnp.sum(grad_out, axis=0)
    scaled = grad_out * norm_gain
    grad_input = inverse * (
        scaled
        - jnp.mean(scaled, axis=-1, keepdims=True)
        - normed * jnp.mean(scaled * normed, axis=-1, keepdims=True)
    )
    return (grad_input, grad_gain, grad_shift)


def split_heads(matrix_rows):
    return matrix_rows.reshape(matrix_rows.shape[0], -1, HDIM)


def merge_heads(head_rows):
    return head_rows.reshape(head_rows.shape[0], -1)


def score_block(queries, key_rows, allowed):
    scores = (
        jnp.einsum(
            "qhd,khd->hqk",
            split_heads(queries),
            split_heads(key_rows),
            preferred_element_type=jnp.float32,
        )
        * scale_dot
    )
    return jnp.where(allowed[None], scores, masked_score)


def attend_forward(queries, key_rows, value_rows, allowed):
    scores = score_block(queries, key_rows, allowed)
    top_score = jnp.max(scores, axis=-1, keepdims=True)
    powers = jnp.exp(scores - top_score)
    totals = jnp.sum(powers, axis=-1, keepdims=True)
    weights = (powers / totals).astype(jnp.bfloat16)
    mixed_rows = jnp.einsum(
        "hqk,khd->qhd", weights, split_heads(value_rows), preferred_element_type=jnp.float32
    )
    return (merge_heads(mixed_rows).astype(jnp.bfloat16), top_score + jnp.log(totals))


def attend_backward(grad_mixed, queries, key_rows, value_rows, allowed, log_totals):
    probs_now = jnp.exp(score_block(queries, key_rows, allowed) - log_totals)
    grad_heads = split_heads(grad_mixed)
    grad_values = jnp.einsum(
        "hqk,qhd->khd",
        probs_now.astype(jnp.bfloat16),
        grad_heads,
        preferred_element_type=jnp.float32,
    )
    grad_probs = jnp.einsum(
        "qhd,khd->hqk", grad_heads, split_heads(value_rows), preferred_element_type=jnp.float32
    )
    weighted = jnp.sum(probs_now * grad_probs, axis=-1, keepdims=True)
    grad_scores = (probs_now * (grad_probs - weighted)).astype(jnp.bfloat16)
    grad_queries = (
        jnp.einsum(
            "hqk,khd->qhd", grad_scores, split_heads(key_rows), preferred_element_type=jnp.float32
        )
        * scale_dot
    )
    grad_keys = (
        jnp.einsum(
            "hqk,qhd->khd", grad_scores, split_heads(queries), preferred_element_type=jnp.float32
        )
        * scale_dot
    )
    return (
        merge_heads(grad_queries).astype(jnp.bfloat16),
        merge_heads(grad_keys).astype(jnp.bfloat16),
        merge_heads(grad_values).astype(jnp.bfloat16),
    )


def attend_sublayer(
    residual, queries, key_rows, value_rows, out_weight, out_bias, norm_gain, norm_shift, allowed
):
    mixed_rows, log_totals = attend_forward(queries, key_rows, value_rows, allowed)
    branch = low_dot(mixed_rows, out_weight) + out_bias
    normed_out, norm_saved = norm_forward(residual + branch, norm_gain, norm_shift)
    return (normed_out, (queries, key_rows, value_rows, log_totals, mixed_rows, norm_saved))


def attend_sublayer_back(grad_out, out_weight, norm_gain, allowed, stored):
    queries, key_rows, value_rows, log_totals, mixed_rows, norm_saved = stored
    grad_sum, grad_gain, grad_shift = norm_backward(grad_out, norm_gain, norm_saved)
    grad_branch = grad_sum.astype(jnp.bfloat16)
    grad_mixed = right_inner(grad_branch, out_weight).astype(jnp.bfloat16)
    grad_queries, grad_keys, grad_values = attend_backward(
        grad_mixed, queries, key_rows, value_rows, allowed, log_totals
    )
    extras = (rows_inner(mixed_rows, grad_branch), column_sum(grad_branch), grad_gain, grad_shift)
    return (grad_sum, grad_queries, grad_keys, grad_values, extras)


def feed_forward(residual, up_weight, up_bias, down_weight, down_bias, norm_gain, norm_shift):
    inputs_low = residual.astype(jnp.bfloat16)
    hidden = low_dot(inputs_low, up_weight) + up_bias
    active = smooth_gate(hidden).astype(jnp.bfloat16)
    branch = low_dot(active, down_weight) + down_bias
    normed_out, norm_saved = norm_forward(residual + branch, norm_gain, norm_shift)
    return (normed_out, (inputs_low, hidden, active, norm_saved))


def feed_back(grad_out, up_weight, down_weight, norm_gain, stored):
    inputs_low, hidden, active, norm_saved = stored
    grad_sum, grad_gain, grad_shift = norm_backward(grad_out, norm_gain, norm_saved)
    grad_branch = grad_sum.astype(jnp.bfloat16)
    grad_active = right_inner(grad_branch, down_weight)
    gate_value, gate_pull = jax.vjp(smooth_gate, hidden)
    grad_hidden = gate_pull(grad_active)[0].astype(jnp.bfloat16)
    grad_input = grad_sum + right_inner(grad_hidden, up_weight)
    grads = (
        rows_inner(inputs_low, grad_hidden),
        column_sum(grad_hidden),
        rows_inner(active, grad_branch),
        column_sum(grad_branch),
        grad_gain,
        grad_shift,
    )
    return (grad_input, grads)


def row_masks(source_seg, target_seg):
    same_source = source_seg[:, None] == source_seg[None, :]
    same_target = target_seg[:, None] == target_seg[None, :]
    same_cross = target_seg[:, None] == source_seg[None, :]
    return (same_source, same_target, same_cross)


def language_rows(target_seg, language_row):
    seg_hot = (
        target_seg[:, None] == jnp.arange(language_row.shape[0], dtype=jnp.int32)[None, :]
    ).astype(jnp.float32)
    lang_hot = (language_row[:, None] == jnp.arange(LANGS, dtype=jnp.int32)[None, :]).astype(
        jnp.float32
    )
    return jnp.dot(seg_hot, lang_hot, precision=highest, preferred_element_type=jnp.float32)


def encoder_forward(enc_whole, source_row, same_source):
    qkv_weight, out_weight, up_weight, down_weight, vectors, up_bias = enc_whole
    columns = vectors.astype(jnp.float32)
    model_width = qkv_weight.shape[0]
    qkv_bias = jnp.concatenate(
        [columns[:, 0], jnp.zeros((model_width,), jnp.float32), columns[:, 1]]
    )
    qkv_rows = project(source_row, qkv_weight, qkv_bias)
    first_out, attend_stored = attend_sublayer(
        source_row.astype(jnp.float32),
        qkv_rows[:, :model_width],
        qkv_rows[:, model_width : 2 * model_width],
        qkv_rows[:, 2 * model_width :],
        out_weight,
        columns[:, 2],
        columns[:, 3],
        columns[:, 4],
        same_source,
    )
    encoded, feed_stored = feed_forward(
        first_out,
        up_weight,
        up_bias.astype(jnp.float32),
        down_weight,
        columns[:, 5],
        columns[:, 6],
        columns[:, 7],
    )
    return (encoded, (source_row, attend_stored, feed_stored))


def encoder_backward(enc_whole, grad_encoded, same_source, stored):
    qkv_weight, out_weight, up_weight, down_weight, vectors, up_bias = enc_whole
    columns = vectors.astype(jnp.float32)
    source_low, attend_stored, feed_stored = stored
    grad_first, feed_grads = feed_back(
        grad_encoded, up_weight, down_weight, columns[:, 6], feed_stored
    )
    grad_sum, grad_queries, grad_keys, grad_values, extras = attend_sublayer_back(
        grad_first, out_weight, columns[:, 3], same_source, attend_stored
    )
    grad_qkv = jnp.concatenate([grad_queries, grad_keys, grad_values], axis=1)
    grad_source = grad_sum + right_inner(grad_qkv, qkv_weight)
    vector_grads = jnp.stack(
        [
            column_sum(grad_queries),
            column_sum(grad_values),
            extras[1],
            extras[2],
            extras[3],
            feed_grads[3],
            feed_grads[4],
            feed_grads[5],
        ],
        axis=1,
    )
    grads = (
        rows_inner(source_low, grad_qkv),
        extras[0],
        feed_grads[0],
        feed_grads[2],
        vector_grads,
        feed_grads[1],
    )
    return (grads, grad_source)


def decoder_forward(dec_whole, target_row, encoded_low, token_language, masks):
    (
        qkv_weight,
        out_weight,
        query_weight,
        memory_weight,
        cross_weight,
        up_weight,
        down_weight,
        vectors,
        up_bias,
        language_table,
    ) = dec_whole
    same_source, same_target, same_cross = masks
    columns = vectors.astype(jnp.float32)
    model_width = qkv_weight.shape[0]
    target_in = target_row.astype(jnp.float32) + right_inner(
        token_language.astype(jnp.bfloat16), language_table
    )
    target_low = target_in.astype(jnp.bfloat16)
    qkv_bias = jnp.concatenate(
        [columns[:, 0], jnp.zeros((model_width,), jnp.float32), columns[:, 1]]
    )
    qkv_rows = project(target_low, qkv_weight, qkv_bias)
    first_out, self_stored = attend_sublayer(
        target_in,
        qkv_rows[:, :model_width],
        qkv_rows[:, model_width : 2 * model_width],
        qkv_rows[:, 2 * model_width :],
        out_weight,
        columns[:, 2],
        columns[:, 3],
        columns[:, 4],
        same_target,
    )
    first_low = first_out.astype(jnp.bfloat16)
    queries = project(first_low, query_weight, columns[:, 5])
    memory = project(
        encoded_low,
        memory_weight,
        jnp.concatenate([jnp.zeros((model_width,), jnp.float32), columns[:, 6]]),
    )
    second_out, cross_stored = attend_sublayer(
        first_out,
        queries,
        memory[:, :model_width],
        memory[:, model_width:],
        cross_weight,
        columns[:, 7],
        columns[:, 8],
        columns[:, 9],
        same_cross,
    )
    output, feed_stored = feed_forward(
        second_out,
        up_weight,
        up_bias.astype(jnp.float32),
        down_weight,
        columns[:, 10],
        columns[:, 11],
        columns[:, 12],
    )
    return (output, (target_low, first_low, self_stored, cross_stored, feed_stored))


def decoder_backward(dec_whole, grad_output, encoded_low, token_language, masks, stored):
    (
        qkv_weight,
        out_weight,
        query_weight,
        memory_weight,
        cross_weight,
        up_weight,
        down_weight,
        vectors,
        up_bias,
        language_table,
    ) = dec_whole
    same_source, same_target, same_cross = masks
    columns = vectors.astype(jnp.float32)
    target_low, first_low, self_stored, cross_stored, feed_stored = stored
    grad_second, feed_grads = feed_back(
        grad_output, up_weight, down_weight, columns[:, 11], feed_stored
    )
    cross_sum, cross_queries, cross_keys, cross_values, cross_extras = attend_sublayer_back(
        grad_second, cross_weight, columns[:, 8], same_cross, cross_stored
    )
    grad_memory = jnp.concatenate([cross_keys, cross_values], axis=1)
    grad_first = cross_sum + right_inner(cross_queries, query_weight)
    grad_encoded = right_inner(grad_memory, memory_weight)
    self_sum, self_queries, self_keys, self_values, self_extras = attend_sublayer_back(
        grad_first, out_weight, columns[:, 3], same_target, self_stored
    )
    grad_qkv = jnp.concatenate([self_queries, self_keys, self_values], axis=1)
    grad_target_in = self_sum + right_inner(grad_qkv, qkv_weight)
    vector_grads = jnp.stack(
        [
            column_sum(self_queries),
            column_sum(self_values),
            self_extras[1],
            self_extras[2],
            self_extras[3],
            column_sum(cross_queries),
            column_sum(cross_values),
            cross_extras[1],
            cross_extras[2],
            cross_extras[3],
            feed_grads[3],
            feed_grads[4],
            feed_grads[5],
        ],
        axis=1,
    )
    grad_language = lax.dot_general(
        grad_target_in,
        token_language,
        (((0,), (0,)), ((), ())),
        precision=highest,
        preferred_element_type=jnp.float32,
    )
    grads = (
        rows_inner(target_low, grad_qkv),
        self_extras[0],
        rows_inner(first_low, cross_queries),
        rows_inner(encoded_low, grad_memory),
        cross_extras[0],
        feed_grads[0],
        feed_grads[2],
        vector_grads,
        feed_grads[1],
        grad_language,
    )
    return (grads, grad_target_in, grad_encoded)


def add_grads(running, fresh):
    return tuple((left_part + right_part for left_part, right_part in zip(running, fresh)))


def shards(
    source,
    target,
    source_segments,
    target_segments,
    target_language,
    cotangent,
    enc_qkv,
    enc_out,
    enc_up,
    enc_down,
    enc_vecs,
    enc_bias_up,
    dec_qkv,
    dec_out,
    cross_q,
    cross_kv,
    cross_out,
    dec_up,
    dec_down,
    dec_vecs,
    dec_bias_up,
    lang_table,
):
    enc_whole = (
        lax.all_gather(enc_qkv, ("dp", "fsdp"), axis=0, tiled=True),
        lax.all_gather(enc_out, ("dp", "fsdp"), axis=0, tiled=True),
        lax.all_gather(enc_up, ("dp", "fsdp"), axis=0, tiled=True),
        lax.all_gather(enc_down, ("dp", "fsdp"), axis=0, tiled=True),
        lax.all_gather(enc_vecs, ("dp", "fsdp"), axis=0, tiled=True),
        lax.all_gather(enc_bias_up, ("dp", "fsdp"), axis=0, tiled=True),
    )
    dec_whole = (
        lax.all_gather(dec_qkv, ("dp", "fsdp"), axis=0, tiled=True),
        lax.all_gather(dec_out, ("dp", "fsdp"), axis=0, tiled=True),
        lax.all_gather(cross_q, ("dp", "fsdp"), axis=0, tiled=True),
        lax.all_gather(cross_kv, ("dp", "fsdp"), axis=0, tiled=True),
        lax.all_gather(cross_out, ("dp", "fsdp"), axis=0, tiled=True),
        lax.all_gather(dec_up, ("dp", "fsdp"), axis=0, tiled=True),
        lax.all_gather(dec_down, ("dp", "fsdp"), axis=0, tiled=True),
        lax.all_gather(dec_vecs, ("dp", "fsdp"), axis=0, tiled=True),
        lax.all_gather(dec_bias_up, ("dp", "fsdp"), axis=0, tiled=True),
        lax.all_gather(lang_table, ("dp", "fsdp"), axis=0, tiled=True),
    )
    row_count, length = source_segments.shape
    model_width = source.shape[1]
    source_rows = source.reshape(row_count, length, model_width)
    target_rows = target.reshape(row_count, length, model_width)
    grad_rows = cotangent.reshape(row_count, length, model_width)
    stored_rows = []
    dec_outputs = []
    for row_index in range(row_count):
        masks = row_masks(source_segments[row_index], target_segments[row_index])
        token_language = language_rows(target_segments[row_index], target_language[row_index])
        encoded, enc_stored = encoder_forward(enc_whole, source_rows[row_index], masks[0])
        encoded_low = encoded.astype(jnp.bfloat16)
        output, dec_stored = decoder_forward(
            dec_whole, target_rows[row_index], encoded_low, token_language, masks
        )
        dec_outputs.append(output.astype(jnp.bfloat16))
        stored_rows.append((masks, token_language, encoded_low, enc_stored, dec_stored))
    enc_again = (
        lax.all_gather(enc_qkv, ("dp", "fsdp"), axis=0, tiled=True),
        lax.all_gather(enc_out, ("dp", "fsdp"), axis=0, tiled=True),
        lax.all_gather(enc_up, ("dp", "fsdp"), axis=0, tiled=True),
        lax.all_gather(enc_down, ("dp", "fsdp"), axis=0, tiled=True),
        lax.all_gather(enc_vecs, ("dp", "fsdp"), axis=0, tiled=True),
        lax.all_gather(enc_bias_up, ("dp", "fsdp"), axis=0, tiled=True),
    )
    dec_again = (
        lax.all_gather(dec_qkv, ("dp", "fsdp"), axis=0, tiled=True),
        lax.all_gather(dec_out, ("dp", "fsdp"), axis=0, tiled=True),
        lax.all_gather(cross_q, ("dp", "fsdp"), axis=0, tiled=True),
        lax.all_gather(cross_kv, ("dp", "fsdp"), axis=0, tiled=True),
        lax.all_gather(cross_out, ("dp", "fsdp"), axis=0, tiled=True),
        lax.all_gather(dec_up, ("dp", "fsdp"), axis=0, tiled=True),
        lax.all_gather(dec_down, ("dp", "fsdp"), axis=0, tiled=True),
        lax.all_gather(dec_vecs, ("dp", "fsdp"), axis=0, tiled=True),
        lax.all_gather(dec_bias_up, ("dp", "fsdp"), axis=0, tiled=True),
        lax.all_gather(lang_table, ("dp", "fsdp"), axis=0, tiled=True),
    )
    target_grads = []
    encoded_grads = []
    dec_total = ()
    for row_index in range(row_count):
        masks, token_language, encoded_low, enc_stored, dec_stored = stored_rows[row_index]
        row_grads, grad_target_in, grad_encoded = decoder_backward(
            dec_again,
            grad_rows[row_index].astype(jnp.float32),
            encoded_low,
            token_language,
            masks,
            dec_stored,
        )
        dec_total = row_grads if row_index == 0 else add_grads(dec_total, row_grads)
        target_grads.append(grad_target_in.astype(jnp.bfloat16))
        encoded_grads.append(grad_encoded)
    (
        grad_dec_qkv,
        grad_dec_out,
        grad_cross_q,
        grad_cross_kv,
        grad_cross_out,
        grad_dec_up,
        grad_dec_down,
        grad_dec_vecs,
        grad_dec_bias_up,
        grad_lang,
    ) = dec_total
    dec_shard_grads = (
        lax.psum_scatter(grad_dec_qkv, ("dp", "fsdp"), scatter_dimension=0, tiled=True),
        lax.psum_scatter(grad_dec_out, ("dp", "fsdp"), scatter_dimension=0, tiled=True),
        lax.psum_scatter(grad_cross_q, ("dp", "fsdp"), scatter_dimension=0, tiled=True),
        lax.psum_scatter(grad_cross_kv, ("dp", "fsdp"), scatter_dimension=0, tiled=True),
        lax.psum_scatter(grad_cross_out, ("dp", "fsdp"), scatter_dimension=0, tiled=True),
        lax.psum_scatter(grad_dec_up, ("dp", "fsdp"), scatter_dimension=0, tiled=True),
        lax.psum_scatter(grad_dec_down, ("dp", "fsdp"), scatter_dimension=0, tiled=True),
        lax.psum_scatter(grad_dec_vecs, ("dp", "fsdp"), scatter_dimension=0, tiled=True),
        lax.psum_scatter(grad_dec_bias_up, ("dp", "fsdp"), scatter_dimension=0, tiled=True),
        lax.psum_scatter(grad_lang, ("dp", "fsdp"), scatter_dimension=0, tiled=True),
    )
    source_grads = []
    enc_total = ()
    for row_index in range(row_count):
        masks, token_language, encoded_low, enc_stored, dec_stored = stored_rows[row_index]
        row_grads, grad_source = encoder_backward(
            enc_again, encoded_grads[row_index], masks[0], enc_stored
        )
        enc_total = row_grads if row_index == 0 else add_grads(enc_total, row_grads)
        source_grads.append(grad_source.astype(jnp.bfloat16))
    grad_enc_qkv, grad_enc_out, grad_enc_up, grad_enc_down, grad_enc_vecs, grad_enc_bias_up = (
        enc_total
    )
    enc_shard_grads = (
        lax.psum_scatter(grad_enc_qkv, ("dp", "fsdp"), scatter_dimension=0, tiled=True),
        lax.psum_scatter(grad_enc_out, ("dp", "fsdp"), scatter_dimension=0, tiled=True),
        lax.psum_scatter(grad_enc_up, ("dp", "fsdp"), scatter_dimension=0, tiled=True),
        lax.psum_scatter(grad_enc_down, ("dp", "fsdp"), scatter_dimension=0, tiled=True),
        lax.psum_scatter(grad_enc_vecs, ("dp", "fsdp"), scatter_dimension=0, tiled=True),
        lax.psum_scatter(grad_enc_bias_up, ("dp", "fsdp"), scatter_dimension=0, tiled=True),
    )
    (
        shard_enc_qkv,
        shard_enc_out,
        shard_enc_up,
        shard_enc_down,
        shard_enc_vecs,
        shard_enc_bias_up,
    ) = enc_shard_grads
    (
        shard_dec_qkv,
        shard_dec_out,
        shard_cross_q,
        shard_cross_kv,
        shard_cross_out,
        shard_dec_up,
        shard_dec_down,
        shard_dec_vecs,
        shard_dec_bias_up,
        shard_lang,
    ) = dec_shard_grads
    return (
        jnp.concatenate(dec_outputs, axis=0),
        jnp.concatenate(source_grads, axis=0),
        jnp.concatenate(target_grads, axis=0),
        shard_enc_qkv,
        shard_enc_out,
        shard_enc_up,
        shard_enc_down,
        shard_enc_vecs,
        shard_enc_bias_up,
        shard_dec_qkv,
        shard_dec_out,
        shard_cross_q,
        shard_cross_kv,
        shard_cross_out,
        shard_dec_up,
        shard_dec_down,
        shard_dec_vecs,
        shard_dec_bias_up,
        shard_lang,
    )


def solution(mesh):
    return jax.shard_map(
        shards,
        mesh=mesh,
        in_specs=(
            P(("dp", "fsdp"), None),
            P(("dp", "fsdp"), None),
            P(("dp", "fsdp"), None),
            P(("dp", "fsdp"), None),
            P(("dp", "fsdp"), None),
            P(("dp", "fsdp"), None),
            P(("dp", "fsdp"), None),
            P(("dp", "fsdp"), None),
            P(("dp", "fsdp"), None),
            P(("dp", "fsdp"), None),
            P(("dp", "fsdp"), None),
            P(("dp", "fsdp")),
            P(("dp", "fsdp"), None),
            P(("dp", "fsdp"), None),
            P(("dp", "fsdp"), None),
            P(("dp", "fsdp"), None),
            P(("dp", "fsdp"), None),
            P(("dp", "fsdp"), None),
            P(("dp", "fsdp"), None),
            P(("dp", "fsdp"), None),
            P(("dp", "fsdp")),
            P(("dp", "fsdp"), None),
        ),
        out_specs=(
            P(("dp", "fsdp"), None),
            P(("dp", "fsdp"), None),
            P(("dp", "fsdp"), None),
            P(("dp", "fsdp"), None),
            P(("dp", "fsdp"), None),
            P(("dp", "fsdp"), None),
            P(("dp", "fsdp"), None),
            P(("dp", "fsdp"), None),
            P(("dp", "fsdp")),
            P(("dp", "fsdp"), None),
            P(("dp", "fsdp"), None),
            P(("dp", "fsdp"), None),
            P(("dp", "fsdp"), None),
            P(("dp", "fsdp"), None),
            P(("dp", "fsdp"), None),
            P(("dp", "fsdp"), None),
            P(("dp", "fsdp"), None),
            P(("dp", "fsdp")),
            P(("dp", "fsdp"), None),
        ),
        check_vma=False,
    )
```

profile of v0, /device:TPU:0, one launch (start us, length us, event | category | flops | bytes accessed | tf_op | source)
XLA Modules:
  0.0 2737.2 jit_solution(14833355787253778781)
XLA Ops:
  14.4 42.2 %all-reduce.6 = (bf16[2048]{0:T(1024)(128)(2,1)S(1)}, bf16[2048]{0:T(1024)(128)(2,1)S(1)}) all-reduce(bf16[2048]{0:T(1024)(128)(2,1)S(1)} %dynamic-update-slice, bf16[2048]{0:T(1024)(128)(2,1)S(1)} %dynamic-update-slice.1), channel_id=1, replica_groups=mesh['dp'=8,'fsdp'=4] {'dp','fsdp'}, use_global_device_ids=true, to_apply=%add.1 | all-reduce | flops 4096 | bytes 16384
  59.4 66.7 %all-gather.1 = bf16[32,16,8]{1,2,0:T(8,128)(2,1)S(1)} all-gather(bf16[1,16,8]{1,2,0:T(8,128)(2,1)} %bitcast.452), channel_id=1, replica_groups=mesh['dp'=8,'fsdp'=4] {'dp','fsdp'}, dimensions={0}, use_global_device_ids=true | all-gather | bytes 8448 | tf_op jit(solution)/shard_map/all_gather | solution.py:431
  126.2 64.3 %all-gather = bf16[32,16,8]{1,2,0:T(8,128)(2,1)S(1)} all-gather(bf16[1,16,8]{1,2,0:T(8,128)(2,1)} %bitcast.453), channel_id=1, replica_groups=mesh['dp'=8,'fsdp'=4] {'dp','fsdp'}, dimensions={0}, use_global_device_ids=true | all-gather | bytes 8448 | tf_op jit(solution)/shard_map/all_gather | solution.py:444
  191.5 67.3 %all_gather.63 = bf16[512,13]{1,0:T(8,128)(2,1)S(1)} all-gather(bf16[16,13]{1,0:T(8,128)(2,1)} %param.41), channel_id=1, replica_groups=mesh['dp'=8,'fsdp'=4] {'dp','fsdp'}, dimensions={0}, use_global_device_ids=true | all-gather | bytes 13728 | tf_op jit(solution)/shard_map/all_gather | solution.py:442
  261.2 69.1 %all_gather.67 = bf16[512,512]{1,0:T(8,128)(2,1)S(1)} all-gather(bf16[16,512]{1,0:T(8,128)(2,1)S(1)} %copy-done.200), channel_id=1, replica_groups=mesh['dp'=8,'fsdp'=4] {'dp','fsdp'}, dimensions={0}, use_global_device_ids=true | all-gather | bytes 540672 | tf_op jit(solution)/shard_map/all_gather | solution.py:428
  330.3 71.1 %all_gather.64 = bf16[512,512]{1,0:T(8,128)(2,1)S(1)} all-gather(bf16[16,512]{1,0:T(8,128)(2,1)S(1)} %copy-done.201), channel_id=1, replica_groups=mesh['dp'=8,'fsdp'=4] {'dp','fsdp'}, dimensions={0}, use_global_device_ids=true | all-gather | bytes 540672 | tf_op jit(solution)/shard_map/all_gather | solution.py:436
  401.3 73.4 %all_gather.72 = bf16[512,512]{1,0:T(8,128)(2,1)} all-gather(bf16[16,512]{1,0:T(8,128)(2,1)S(1)} %copy-done.202), channel_id=1, replica_groups=mesh['dp'=8,'fsdp'=4] {'dp','fsdp'}, dimensions={0}, use_global_device_ids=true | all-gather | bytes 540672 | tf_op jit(solution)/shard_map/all_gather | solution.py:437
  474.7 74.5 %all_gather.73 = bf16[512,512]{1,0:T(8,128)(2,1)} all-gather(bf16[16,512]{1,0:T(8,128)(2,1)S(1)} %copy-done.203), channel_id=1, replica_groups=mesh['dp'=8,'fsdp'=4] {'dp','fsdp'}, dimensions={0}, use_global_device_ids=true | all-gather | bytes 540672 | tf_op jit(solution)/shard_map/all_gather | solution.py:439
  631.2 5.4 fusion.216
  636.7 5.4 fusion.240
  673.3 5.3 fusion.212
  678.7 5.1 fusion.245
  701.5 10.4 convert_reduce_fusion.1
  782.0 5.1 multiply_reduce_fusion.2
  790.5 5.1 multiply_reduce_fusion.4
  827.8 6.7 multiply_convert_fusion.2
  838.1 6.7 multiply_convert_fusion.4
  922.6 4.6 fusion.189
  942.2 38.3 %all-reduce.5 = (f32[2048]{0:T(1024)S(1)}, f32[2048]{0:T(1024)S(1)}) all-reduce(f32[2048]{0:T(1024)S(1)} %add.672, f32[2048]{0:T(1024)S(1)} %add.681), channel_id=7, replica_groups=mesh['dp'=8,'fsdp'=4] {'dp','fsdp'}, use_global_device_ids=true, to_apply=%region_81.82.clone | all-reduce | flops 4096 | bytes 32768
  989.5 123.3 %reduce-scatter.49.cloned.1.call-done = f32[16,8]{1,0:T(8,128)} async-done(((f32[512,8]{1,0:T(8,128)}), f32[16,8]{1,0:T(8,128)}) %reduce-scatter.49.cloned.1.call-update) | async-done | bytes 528
  1114.2 131.1 %reduce-scatter.47.cloned.1.call-done = f32[16,13]{1,0:T(8,128)} async-done(((f32[512,13]{1,0:T(8,128)}), f32[16,13]{1,0:T(8,128)}) %reduce-scatter.47.cloned.1.call-update) | async-done | bytes 848
  1245.3 134.5 %reduce-scatter.37.cloned.1.call-done = f32[16,512]{1,0:T(8,128)} async-done(((f32[512,512]{1,0:T(8,128)}), f32[16,512]{1,0:T(8,128)}) %reduce-scatter.37.cloned.1.call-update) | async-done | bytes 32784 | tf_op jit(solution)/shard_map/reduce_scatter | solution.py:516
  1379.9 134.7 %reduce-scatter.33.cloned.1.call-done = f32[16,512]{1,0:T(8,128)} async-done(((f32[512,512]{1,0:T(8,128)}), f32[16,512]{1,0:T(8,128)}) %reduce-scatter.33.cloned.1.call-update) | async-done | bytes 32784 | tf_op jit(solution)/shard_map/reduce_scatter | solution.py:514
  1514.6 134.6 %reduce-scatter.31.cloned.1.call-done = f32[16,512]{1,0:T(8,128)} async-done(((f32[512,512]{1,0:T(8,128)}), f32[16,512]{1,0:T(8,128)}) %reduce-scatter.31.cloned.1.call-update) | async-done | bytes 32784 | tf_op jit(solution)/shard_map/reduce_scatter | solution.py:513
  1649.2 134.5 %reduce-scatter.23.cloned.1.call-done = f32[16,512]{1,0:T(8,128)} async-done(((f32[512,512]{1,0:T(8,128)}), f32[16,512]{1,0:T(8,128)}) %reduce-scatter.23.cloned.1.call-update) | async-done | bytes 32784 | tf_op jit(solution)/shard_map/reduce_scatter | solution.py:537
  1783.7 137.9 %reduce-scatter.35.cloned.1.call-done = f32[16,1024]{1,0:T(8,128)} async-done(((f32[512,1024]{1,0:T(8,128)}), f32[16,1024]{1,0:T(8,128)}) %reduce-scatter.35.cloned.1.call-update) | async-done | bytes 65552 | tf_op jit(solution)/shard_map/reduce_scatter | solution.py:515
  1921.6 105.2 %reduce-scatter.43.cloned.1.call-done = f32[16,1536]{1,0:T(8,128)} async-done(((f32[512,1536]{1,0:T(8,128)}), f32[16,1536]{1,0:T(8,128)}) %reduce-scatter.43.cloned.1.call-update) | async-done | bytes 98320
  2026.8 106.4 %reduce-scatter.29.cloned.1.call-done = f32[16,1536]{1,0:T(8,128)} async-done(((f32[512,1536]{1,0:T(8,128)}), f32[16,1536]{1,0:T(8,128)}) %reduce-scatter.29.cloned.1.call-update) | async-done | bytes 98320 | tf_op jit(solution)/shard_map/reduce_scatter | solution.py:512
  2133.2 149.0 %reduce-scatter.41.cloned.1.call-done = f32[64,512]{1,0:T(8,128)} async-done(((f32[2048,512]{1,0:T(8,128)}), f32[64,512]{1,0:T(8,128)}) %reduce-scatter.41.cloned.1.call-update) | async-done | bytes 131088 | tf_op jit(solution)/shard_map/reduce_scatter | solution.py:518
  2282.2 148.8 %reduce-scatter.39.cloned.1.call-done = f32[16,2048]{1,0:T(8,128)} async-done(((f32[512,2048]{1,0:T(8,128)}), f32[16,2048]{1,0:T(8,128)}) %reduce-scatter.39.cloned.1.call-update) | async-done | bytes 131088 | tf_op jit(solution)/shard_map/reduce_scatter | solution.py:517
  2431.0 149.4 %reduce-scatter.27.cloned.1.call-done = f32[64,512]{1,0:T(8,128)} async-done(((f32[2048,512]{1,0:T(8,128)}), f32[64,512]{1,0:T(8,128)}) %reduce-scatter.27.cloned.1.call-update) | async-done | bytes 131088 | tf_op jit(solution)/shard_map/reduce_scatter | solution.py:539
  2580.3 149.8 %reduce-scatter.25.cloned.1.call-done = f32[16,2048]{1,0:T(8,128)} async-done(((f32[512,2048]{1,0:T(8,128)}), f32[16,2048]{1,0:T(8,128)}) %reduce-scatter.25.cloned.1.call-update) | async-done | bytes 131088 | tf_op jit(solution)/shard_map/reduce_scatter | solution.py:538
  (854 shorter events, 353.5 us)
Async XLA Ops:
  7.2 254.0 %copy-start.200 = (bf16[16,512]{1,0:T(8,128)(2,1)S(1)}, bf16[16,512]{1,0:T(8,128)(2,1)}, u32[]{:S(2)}) copy-start(bf16[16,512]{1,0:T(8,128)(2,1)} %param.29) | copy-start | bytes 49156
  7.2 323.1 %copy-start.201 = (bf16[16,512]{1,0:T(8,128)(2,1)S(1)}, bf16[16,512]{1,0:T(8,128)(2,1)}, u32[]{:S(2)}) copy-start(bf16[16,512]{1,0:T(8,128)(2,1)} %param.35) | copy-start | bytes 49156
  7.2 394.1 %copy-start.202 = (bf16[16,512]{1,0:T(8,128)(2,1)S(1)}, bf16[16,512]{1,0:T(8,128)(2,1)}, u32[]{:S(2)}) copy-start(bf16[16,512]{1,0:T(8,128)(2,1)} %param.36) | copy-start | bytes 49156
  7.2 467.5 %copy-start.203 = (bf16[16,512]{1,0:T(8,128)(2,1)S(1)}, bf16[16,512]{1,0:T(8,128)(2,1)}, u32[]{:S(2)}) copy-start(bf16[16,512]{1,0:T(8,128)(2,1)} %param.38) | copy-start | bytes 49156
  7.2 562.1 %all-gather.10.cloned.1.call-start = ((), (), s32[]{:S(2)}) async-start(), calls=%async_computation.14 | async-start | bytes 1622016 | tf_op jit(solution)/shard_map/all_gather | solution.py:435
  8.0 576.9 %all-gather.12.cloned.1.call-start = ((), (), s32[]{:S(2)}) async-start(), calls=%async_computation.15 | async-start | bytes 1622016 | tf_op jit(solution)/shard_map/all_gather | solution.py:427
  8.7 622.5 %all-gather.14.cloned.1.call-start = ((), (), s32[]{:S(2)}) async-start(), calls=%async_computation.16 | async-start | bytes 2162688 | tf_op jit(solution)/shard_map/all_gather | solution.py:429
  9.4 627.2 %all-gather.16.cloned.1.call-start = ((), (), s32[]{:S(2)}) async-start(), calls=%async_computation.17 | async-start | bytes 2162688 | tf_op jit(solution)/shard_map/all_gather | solution.py:430
  10.0 637.6 %all-gather.18.cloned.1.call-start = ((), (), s32[]{:S(2)}) async-start(), calls=%async_computation.18 | async-start | bytes 1081344 | tf_op jit(solution)/shard_map/all_gather | solution.py:438
  10.6 662.7 %all-gather.20.cloned.1.call-start = ((), (), s32[]{:S(2)}) async-start(), calls=%async_computation.19 | async-start | bytes 2162688 | tf_op jit(solution)/shard_map/all_gather | solution.py:440
  11.2 667.5 %all-gather.22.cloned.1.call-start = ((), (), s32[]{:S(2)}) async-start(), calls=%async_computation.20 | async-start | bytes 2162688 | tf_op jit(solution)/shard_map/all_gather | solution.py:441
  11.9 976.2 %reduce-scatter.45.cloned.1.call-start = ((), (), s32[]{:S(2)}) async-start(), calls=%async_computation.32 | async-start | bytes 270336
  191.5 452.2 %copy-start.161 = (f32[512,1]{0,1:T(1,128)}, f32[512,1]{0,1:T(1,128)S(1)}, u32[]{:S(2)}) copy-start(f32[512,1]{0,1:T(1,128)S(1)} %get-tuple-element.201) | copy-start | bytes 6148
  191.5 458.7 %copy-start.193 = (f32[512,1]{0,1:T(1,128)}, f32[512,1]{0,1:T(1,128)S(1)}, u32[]{:S(2)}) copy-start(f32[512,1]{0,1:T(1,128)S(1)} %get-tuple-element.199) | copy-start | bytes 6148
  261.2 427.6 %copy-start.190 = (f32[512]{0:T(512)}, f32[512]{0:T(512)S(1)}, u32[]{:S(2)}) copy-start(f32[512]{0:T(512)S(1)} %get-tuple-element.141) | copy-start | bytes 6148
  261.2 431.2 %copy-start.159 = (f32[512]{0:T(512)}, f32[512]{0:T(512)S(1)}, u32[]{:S(2)}) copy-start(f32[512]{0:T(512)S(1)} %get-tuple-element.136) | copy-start | bytes 6148
  261.2 458.6 %copy-start.157 = (f32[512]{0:T(512)}, f32[512]{0:T(512)S(1)}, u32[]{:S(2)}) copy-start(f32[512]{0:T(512)S(1)} %get-tuple-element.137) | copy-start | bytes 6148
  330.3 281.6 %copy-start.28 = (bf16[512,512]{1,0:T(8,128)(2,1)}, bf16[512,512]{1,0:T(8,128)(2,1)S(1)}, u32[]{:S(2)}) copy-start(bf16[512,512]{1,0:T(8,128)(2,1)S(1)} %all_gather.67) | copy-start | bytes 1572868
  401.3 217.8 %copy-start.30 = (bf16[512,512]{1,0:T(8,128)(2,1)}, bf16[512,512]{1,0:T(8,128)(2,1)S(1)}, u32[]{:S(2)}) copy-start(bf16[512,512]{1,0:T(8,128)(2,1)S(1)} %all_gather.64) | copy-start | bytes 1572868
  849.6 263.3 %reduce-scatter.49.cloned.1.call-start = ((), (), s32[]{:S(2)}) async-start(), calls=%async_computation.34 | async-start | bytes 270336
  858.7 386.6 %reduce-scatter.47.cloned.1.call-start = ((), (), s32[]{:S(2)}) async-start(), calls=%async_computation.33 | async-start | bytes 270336
  863.2 516.7 %reduce-scatter.37.cloned.1.call-start = ((), (), s32[]{:S(2)}) async-start(), calls=%async_computation.28 | async-start | bytes 1081344 | tf_op jit(solution)/shard_map/reduce_scatter | solution.py:516
  866.4 648.2 %reduce-scatter.33.cloned.1.call-start = ((), (), s32[]{:S(2)}) async-start(), calls=%async_computation.26 | async-start | bytes 1081344 | tf_op jit(solution)/shard_map/reduce_scatter | solution.py:514
  870.7 778.5 %reduce-scatter.31.cloned.1.call-start = ((), (), s32[]{:S(2)}) async-start(), calls=%async_computation.25 | async-start | bytes 1081344 | tf_op jit(solution)/shard_map/reduce_scatter | solution.py:513
  875.1 908.6 %reduce-scatter.23.cloned.1.call-start = ((), (), s32[]{:S(2)}) async-start(), calls=%async_computation.21 | async-start | bytes 1081344 | tf_op jit(solution)/shard_map/reduce_scatter | solution.py:537
  880.1 1041.5 %reduce-scatter.35.cloned.1.call-start = ((), (), s32[]{:S(2)}) async-start(), calls=%async_computation.27 | async-start | bytes 2162688 | tf_op jit(solution)/shard_map/reduce_scatter | solution.py:515
  884.5 1142.3 %reduce-scatter.43.cloned.1.call-start = ((), (), s32[]{:S(2)}) async-start(), calls=%async_computation.31 | async-start | bytes 3244032
  899.3 1233.9 %reduce-scatter.29.cloned.1.call-start = ((), (), s32[]{:S(2)}) async-start(), calls=%async_computation.24 | async-start | bytes 3244032 | tf_op jit(solution)/shard_map/reduce_scatter | solution.py:512
  904.9 1377.3 %reduce-scatter.41.cloned.1.call-start = ((), (), s32[]{:S(2)}) async-start(), calls=%async_computation.30 | async-start | bytes 4325376 | tf_op jit(solution)/shard_map/reduce_scatter | solution.py:518
  913.8 1517.2 %reduce-scatter.39.cloned.1.call-start = ((), (), s32[]{:S(2)}) async-start(), calls=%async_computation.29 | async-start | bytes 4325376 | tf_op jit(solution)/shard_map/reduce_scatter | solution.py:517
  921.4 1658.9 %reduce-scatter.27.cloned.1.call-start = ((), (), s32[]{:S(2)}) async-start(), calls=%async_computation.23 | async-start | bytes 4325376 | tf_op jit(solution)/shard_map/reduce_scatter | solution.py:539
  931.7 1798.4 %reduce-scatter.25.cloned.1.call-start = ((), (), s32[]{:S(2)}) async-start(), calls=%async_computation.22 | async-start | bytes 4325376 | tf_op jit(solution)/shard_map/reduce_scatter | solution.py:538
  (258 other events, 2044.0 us)
Sparse Core Ops, SparseCore 0:
  10.9 57.7 all-gather.9
  71.6 53.9 all-gather.11
  128.5 55.3 all-gather.13
  186.8 55.4 all-gather.15
  245.1 52.8 all-gather.17
  300.8 56.0 all-gather.19
  359.8 55.5 all-gather.21
  849.7 131.0 reduce-scatter.44
  983.1 129.6 reduce-scatter.48
  1115.5 129.7 reduce-scatter.46
  1248.2 131.5 reduce-scatter.36
  1382.5 132.0 reduce-scatter.32
  1517.5 131.6 reduce-scatter.30
  1651.9 131.7 reduce-scatter.22
  1786.5 135.0 reduce-scatter.34
  1927.5 99.2 reduce-scatter.42
  2032.6 100.5 reduce-scatter.28
  2135.9 146.2 reduce-scatter.40
  2285.1 145.8 reduce-scatter.38
  2433.7 146.6 reduce-scatter.26
  2583.2 146.8 reduce-scatter.24
where the time goes:
time: 2740 us
  waiting for transfers between devices  1740 us (64%)
  blocking collectives  567 us (21%)
  matrix products  254 us (9%)
  local copies, waits for them, and re-layouts  94 us (3%)
  other arithmetic  58.8 us (2%)
    unnamed x25, waiting for transfers between devices  364 us
    reduce_scatter x1, waiting for transfers between devices, shards(): lax.psum_scatter(grad_enc_up, ('dp', 'fsdp'), scatter_dimension=0, tiled=...  150 us
    reduce_scatter x1, waiting for transfers between devices, shards(): lax.psum_scatter(grad_enc_down, ('dp', 'fsdp'), scatter_dimension=0, tile...  149 us
    reduce_scatter x1, waiting for transfers between devices, shards(): lax.psum_scatter(grad_dec_down, ('dp', 'fsdp'), scatter_dimension=0, tile...  149 us
    reduce_scatter x1, waiting for transfers between devices, shards(): lax.psum_scatter(grad_dec_up, ('dp', 'fsdp'), scatter_dimension=0, tiled=...  149 us
    reduce_scatter x1, waiting for transfers between devices, shards(): lax.psum_scatter(grad_cross_kv, ('dp', 'fsdp'), scatter_dimension=0, tile...  138 us
    reduce_scatter x1, waiting for transfers between devices, shards(): lax.psum_scatter(grad_cross_q, ('dp', 'fsdp'), scatter_dimension=0, tiled...  135 us
    reduce_scatter x1, waiting for transfers between devices, shards(): lax.psum_scatter(grad_dec_out, ('dp', 'fsdp'), scatter_dimension=0, tiled...  135 us
  transfers between devices with their start and end apart: 21, of which 13 were waited for; matrix products, arithmetic and copies ran while one was open for 8% of the time, Pallas kernels for 0%

commit v1 on v0

--- a/solution.py
+++ b/solution.py
@@ -1,6 +1,10 @@
+import functools
+
 import jax
 import jax.numpy as jnp
 from jax import lax
+from jax.experimental import pallas as pl
+from jax.experimental.pallas import tpu as pltpu
 from jax.sharding import PartitionSpec as P
 
 HDIM = 64
@@ -395,11 +399,169 @@
     return (grads, grad_target_in, grad_encoded)
 
 
+AXES = ("dp", "fsdp")
+
+
+class Grid:
+    def __init__(self, mesh):
+        self.nd = mesh.shape["dp"]
+        self.nf = mesh.shape["fsdp"]
+        self.n = self.nd * self.nf
+        self.nh = self.nd // 2
+        self.bits = [1 << b for b in range(1, self.nd.bit_length() - 1)]
+
+    def me(self):
+        return lax.axis_index("dp") * self.nf + lax.axis_index("fsdp")
+
+    def swap_dp(self, value, flip):
+        return lax.ppermute(value, "dp", [(i, i ^ flip) for i in range(self.nd)])
+
+    def swap_fsdp(self, value, flip):
+        return lax.ppermute(value, "fsdp", [(i, i ^ flip) for i in range(self.nf)])
+
+
+def gather_relative(grid, shard, flipped):
+    parts = [shard] + [grid.swap_fsdp(shard, m) for m in range(1, grid.nf)]
+    held = jnp.stack(parts)[None]
+    bits = list(reversed(grid.bits)) if flipped else grid.bits
+    order = [0]
+    for bit in bits:
+        held = jnp.concatenate([held, grid.swap_dp(held, bit)], axis=0)
+        order = order + [o | bit for o in order]
+    held = held.reshape((-1,) + shard.shape)
+    other = grid.swap_dp(held, 1)
+    return held, other, [o >> 1 for o in order]
+
+
+def scatter_relative(grid, keep, send, flipped):
+    rows = keep.shape[1:]
+    got = grid.swap_dp(send, 1)
+    held = keep.astype(jnp.float32) + got.astype(jnp.float32)
+    held = held.reshape((grid.nh, grid.nf) + rows)
+    bits = list(reversed(grid.bits)) if flipped else grid.bits
+    for bit in reversed(bits):
+        half = held.shape[0] // 2
+        held = held[:half] + grid.swap_dp(held[half:].astype(jnp.bfloat16), bit).astype(jnp.float32)
+    held = held[0]
+    total = held[0]
+    for m in range(1, grid.nf):
+        total = total + grid.swap_fsdp(held[m].astype(jnp.bfloat16), m).astype(jnp.float32)
+    return total
+
+
+def spread_order(grid, flipped):
+    bits = list(reversed(grid.bits)) if flipped else grid.bits
+    order = [0]
+    for bit in bits:
+        order = order + [o | bit for o in order]
+    return [o >> 1 for o in order]
+
+
 def add_grads(running, fresh):
     return tuple((left_part + right_part for left_part, right_part in zip(running, fresh)))
 
 
+def place_kernel(order, nf, forms, me_ref, mine, other, *refs):
+    outs, sem = refs[:-1], refs[-1]
+    me = me_ref[0]
+    copies = []
+    for part, source in enumerate((mine, other)):
+        for at in range(len(order) * nf):
+            r = (order[at // nf] * 2 + part) * nf + at % nf
+            i = jnp.bitwise_xor(me, r)
+            row = 0
+            for out, (blocks, wide) in zip(outs, forms):
+                dst = out.at[:, i] if wide else out.at[i]
+                copies.append(
+                    pltpu.make_async_copy(source.at[at, pl.ds(row, blocks)], dst, sem)
+                )
+                row += blocks
+    for copy in copies:
+        copy.start()
+    for copy in copies:
+        copy.wait()
+
+
+def place_weights(grid, gathered, forms):
+    mine, other, order = gathered
+    rows = mine.shape[1]
+    unit = rows // sum(b for b, _ in forms)
+    me = grid.me()
+    if unit % 16:
+        whole = jnp.concatenate([mine, other])
+        table = [0] * grid.n
+        for part in range(2):
+            for at in range(mine.shape[0]):
+                r = (order[at // grid.nf] * 2 + part) * grid.nf + at % grid.nf
+                table[r] = part * mine.shape[0] + at
+        index = jnp.array(table, jnp.int32)[jnp.arange(grid.n, dtype=jnp.int32) ^ me]
+        whole = jnp.take(whole, index, axis=0)
+        outs, row = [], 0
+        for blocks, wide in forms:
+            part = whole[:, row : row + blocks * unit]
+            if wide:
+                part = part.reshape(grid.n, blocks, unit, 512).transpose(1, 0, 2, 3)
+            outs.append(part.reshape(blocks, 512, 512))
+            row += blocks * unit
+        return outs
+    split = (mine.shape[0], rows // unit, unit, 512)
+    outs = pl.pallas_call(
+        functools.partial(place_kernel, order, grid.nf, forms),
+        out_shape=[
+            jax.ShapeDtypeStruct(
+                (blocks, grid.n, unit, 512) if wide else (grid.n, blocks, unit, 512), jnp.bfloat16
+            )
+            for blocks, wide in forms
+        ],
+        in_specs=[pl.BlockSpec(memory_space=pltpu.SMEM)] + [pl.BlockSpec(memory_space=pl.ANY)] * 2,
+        out_specs=[pl.BlockSpec(memory_space=pl.ANY)] * len(forms),
+        scratch_shapes=[pltpu.SemaphoreType.DMA],
+    )(me.reshape(1), mine.reshape(split), other.reshape(split))
+    return [out.reshape(blocks, 512, 512) for out, (blocks, _) in zip(outs, forms)]
+
+
+def spread_grads(grid, grads, forms, flipped):
+    unit = 512 // grid.n
+    order = spread_order(grid, flipped)
+    me = grid.me()
+    parts = []
+    for grad, (blocks, wide) in zip(grads, forms):
+        if wide:
+            part = grad.reshape(blocks, grid.n, unit, 512).transpose(1, 0, 2, 3)
+        else:
+            part = grad.reshape(grid.n, blocks, unit, 512)
+        parts.append(part.reshape(grid.n, blocks * unit, 512))
+    whole = jnp.concatenate(parts, axis=1)
+    sides = []
+    for part in range(2):
+        table = [
+            (o * 2 + part) * grid.nf + z for o in order for z in range(grid.nf)
+        ]
+        sides.append(jnp.take(whole, jnp.array(table, jnp.int32) ^ me, axis=0))
+    return scatter_relative(grid, sides[0], sides[1], flipped)
+
+
+def to_rows(shard):
+    unit = shard.shape[0]
+    blocks = shard.shape[1] // 512
+    return shard.reshape(unit, blocks, 512).transpose(1, 0, 2).reshape(blocks * unit, 512)
+
+
+def from_rows(rows, blocks):
+    unit = rows.shape[0] // blocks
+    return rows.reshape(blocks, unit, 512).transpose(1, 0, 2).reshape(unit, blocks * 512)
+
+
+def side_by_side(blocks):
+    return jnp.concatenate(list(blocks), axis=1)
+
+
+def to_blocks(grad):
+    return grad.astype(jnp.bfloat16).reshape(512, -1, 512).transpose(1, 0, 2)
+
+
 def shards(
+    grid,
     source,
     target,
     source_segments,
@@ -423,26 +585,51 @@
     dec_bias_up,
     lang_table,
 ):
+    unit = enc_qkv.shape[0]
+    bias_unit = enc_bias_up.shape[0] // unit
+    small = jnp.concatenate(
+        [
+            enc_vecs,
+            dec_vecs,
+            lang_table,
+            enc_bias_up.reshape(unit, bias_unit),
+            dec_bias_up.reshape(unit, bias_unit),
+        ],
+        axis=1,
+    )
+    small = jnp.pad(small, ((0, 0), (0, 512 - small.shape[1])))
+    pieces = (
+        ([to_rows(enc_qkv), small], ((3, True), (1, True))),
+        ([to_rows(enc_out), to_rows(enc_up), enc_down], ((1, True), (4, True), (4, False))),
+        ([to_rows(dec_qkv), to_rows(dec_out), to_rows(cross_q), to_rows(cross_kv), to_rows(cross_out)], ((3, True), (1, True), (1, True), (2, True), (1, True))),
+        ([to_rows(dec_up), dec_down], ((4, True), (4, False))),
+    )
+    placed = []
+    for number, (arrays, forms) in enumerate(pieces):
+        gathered = gather_relative(grid, jnp.concatenate(arrays, axis=0), number % 2 == 1)
+        placed.append(place_weights(grid, gathered, forms))
+    vectors = placed[0][1][0]
     enc_whole = (
-        lax.all_gather(enc_qkv, ("dp", "fsdp"), axis=0, tiled=True),
-        lax.all_gather(enc_out, ("dp", "fsdp"), axis=0, tiled=True),
-        lax.all_gather(enc_up, ("dp", "fsdp"), axis=0, tiled=True),
-        lax.all_gather(enc_down, ("dp", "fsdp"), axis=0, tiled=True),
-        lax.all_gather(enc_vecs, ("dp", "fsdp"), axis=0, tiled=True),
-        lax.all_gather(enc_bias_up, ("dp", "fsdp"), axis=0, tiled=True),
+        side_by_side(placed[0][0]),
+        placed[1][0][0],
+        side_by_side(placed[1][1]),
+        placed[1][2].reshape(-1, 512),
+        vectors[:, :8],
+        vectors[:, 29:33].reshape(-1),
     )
     dec_whole = (
-        lax.all_gather(dec_qkv, ("dp", "fsdp"), axis=0, tiled=True),
-        lax.all_gather(dec_out, ("dp", "fsdp"), axis=0, tiled=True),
-        lax.all_gather(cross_q, ("dp", "fsdp"), axis=0, tiled=True),
-        lax.all_gather(cross_kv, ("dp", "fsdp"), axis=0, tiled=True),
-        lax.all_gather(cross_out, ("dp", "fsdp"), axis=0, tiled=True),
-        lax.all_gather(dec_up, ("dp", "fsdp"), axis=0, tiled=True),
-        lax.all_gather(dec_down, ("dp", "fsdp"), axis=0, tiled=True),
-        lax.all_gather(dec_vecs, ("dp", "fsdp"), axis=0, tiled=True),
-        lax.all_gather(dec_bias_up, ("dp", "fsdp"), axis=0, tiled=True),
-        lax.all_gather(lang_table, ("dp", "fsdp"), axis=0, tiled=True),
-    )
+        side_by_side(placed[2][0]),
+        placed[2][1][0],
+        placed[2][2][0],
+        side_by_side(placed[2][3]),
+        placed[2][4][0],
+        side_by_side(placed[3][0]),
+        placed[3][1].reshape(-1, 512),
+        vectors[:, 8:21],
+        vectors[:, 33:37].reshape(-1),
+        vectors[:, 21:29],
+    )
+    enc_again, dec_again = enc_whole, dec_whole
     row_count, length = source_segments.shape
     model_width = source.shape[1]
     source_rows = source.reshape(row_count, length, model_width)
@@ -460,26 +647,6 @@
         )
         dec_outputs.append(output.astype(jnp.bfloat16))
         stored_rows.append((masks, token_language, encoded_low, enc_stored, dec_stored))
-    enc_again = (
-        lax.all_gather(enc_qkv, ("dp", "fsdp"), axis=0, tiled=True),
-        lax.all_gather(enc_out, ("dp", "fsdp"), axis=0, tiled=True),
-        lax.all_gather(enc_up, ("dp", "fsdp"), axis=0, tiled=True),
-        lax.all_gather(enc_down, ("dp", "fsdp"), axis=0, tiled=True),
-        lax.all_gather(enc_vecs, ("dp", "fsdp"), axis=0, tiled=True),
-        lax.all_gather(enc_bias_up, ("dp", "fsdp"), axis=0, tiled=True),
-    )
-    dec_again = (
-        lax.all_gather(dec_qkv, ("dp", "fsdp"), axis=0, tiled=True),
-        lax.all_gather(dec_out, ("dp", "fsdp"), axis=0, tiled=True),
-        lax.all_gather(cross_q, ("dp", "fsdp"), axis=0, tiled=True),
-        lax.all_gather(cross_kv, ("dp", "fsdp"), axis=0, tiled=True),
-        lax.all_gather(cross_out, ("dp", "fsdp"), axis=0, tiled=True),
-        lax.all_gather(dec_up, ("dp", "fsdp"), axis=0, tiled=True),
-        lax.all_gather(dec_down, ("dp", "fsdp"), axis=0, tiled=True),
-        lax.all_gather(dec_vecs, ("dp", "fsdp"), axis=0, tiled=True),
-        lax.all_gather(dec_bias_up, ("dp", "fsdp"), axis=0, tiled=True),
-        lax.all_gather(lang_table, ("dp", "fsdp"), axis=0, tiled=True),
-    )
     target_grads = []
     encoded_grads = []
     dec_total = ()
@@ -508,17 +675,17 @@
         grad_dec_bias_up,
         grad_lang,
     ) = dec_total
-    dec_shard_grads = (
-        lax.psum_scatter(grad_dec_qkv, ("dp", "fsdp"), scatter_dimension=0, tiled=True),
-        lax.psum_scatter(grad_dec_out, ("dp", "fsdp"), scatter_dimension=0, tiled=True),
-        lax.psum_scatter(grad_cross_q, ("dp", "fsdp"), scatter_dimension=0, tiled=True),
-        lax.psum_scatter(grad_cross_kv, ("dp", "fsdp"), scatter_dimension=0, tiled=True),
-        lax.psum_scatter(grad_cross_out, ("dp", "fsdp"), scatter_dimension=0, tiled=True),
-        lax.psum_scatter(grad_dec_up, ("dp", "fsdp"), scatter_dimension=0, tiled=True),
-        lax.psum_scatter(grad_dec_down, ("dp", "fsdp"), scatter_dimension=0, tiled=True),
-        lax.psum_scatter(grad_dec_vecs, ("dp", "fsdp"), scatter_dimension=0, tiled=True),
-        lax.psum_scatter(grad_dec_bias_up, ("dp", "fsdp"), scatter_dimension=0, tiled=True),
-        lax.psum_scatter(grad_lang, ("dp", "fsdp"), scatter_dimension=0, tiled=True),
+    dec_a = spread_grads(
+        grid,
+        [to_blocks(grad_dec_up), grad_dec_down.astype(jnp.bfloat16).reshape(4, 512, 512)],
+        ((4, True), (4, False)),
+        False,
+    )
+    dec_b = spread_grads(
+        grid,
+        [to_blocks(g) for g in (grad_dec_qkv, grad_dec_out, grad_cross_q, grad_cross_kv, grad_cross_out)],
+        ((3, True), (1, True), (1, True), (2, True), (1, True)),
+        True,
     )
     source_grads = []
     enc_total = ()
@@ -532,34 +699,46 @@
     grad_enc_qkv, grad_enc_out, grad_enc_up, grad_enc_down, grad_enc_vecs, grad_enc_bias_up = (
         enc_total
     )
-    enc_shard_grads = (
-        lax.psum_scatter(grad_enc_qkv, ("dp", "fsdp"), scatter_dimension=0, tiled=True),
-        lax.psum_scatter(grad_enc_out, ("dp", "fsdp"), scatter_dimension=0, tiled=True),
-        lax.psum_scatter(grad_enc_up, ("dp", "fsdp"), scatter_dimension=0, tiled=True),
-        lax.psum_scatter(grad_enc_down, ("dp", "fsdp"), scatter_dimension=0, tiled=True),
-        lax.psum_scatter(grad_enc_vecs, ("dp", "fsdp"), scatter_dimension=0, tiled=True),
-        lax.psum_scatter(grad_enc_bias_up, ("dp", "fsdp"), scatter_dimension=0, tiled=True),
-    )
-    (
-        shard_enc_qkv,
-        shard_enc_out,
-        shard_enc_up,
-        shard_enc_down,
-        shard_enc_vecs,
-        shard_enc_bias_up,
-    ) = enc_shard_grads
-    (
-        shard_dec_qkv,
-        shard_dec_out,
-        shard_cross_q,
-        shard_cross_kv,
-        shard_cross_out,
-        shard_dec_up,
-        shard_dec_down,
-        shard_dec_vecs,
-        shard_dec_bias_up,
-        shard_lang,
-    ) = dec_shard_grads
+    enc_a = spread_grads(
+        grid,
+        [to_blocks(grad_enc_up), grad_enc_down.astype(jnp.bfloat16).reshape(4, 512, 512)],
+        ((4, True), (4, False)),
+        False,
+    )
+    small_grads = jnp.concatenate(
+        [
+            grad_enc_vecs,
+            grad_dec_vecs,
+            grad_lang,
+            grad_enc_bias_up.reshape(512, bias_unit),
+            grad_dec_bias_up.reshape(512, bias_unit),
+        ],
+        axis=1,
+    )
+    small_grads = jnp.pad(small_grads, ((0, 0), (0, 512 - small_grads.shape[1])))
+    enc_b = spread_grads(
+        grid,
+        [to_blocks(g) for g in (grad_enc_qkv, grad_enc_out, small_grads)],
+        ((3, True), (1, True), (1, True)),
+        True,
+    )
+    shard_dec_up = from_rows(dec_a[: 4 * unit], 4)
+    shard_dec_down = dec_a[4 * unit :]
+    shard_dec_qkv = from_rows(dec_b[: 3 * unit], 3)
+    shard_dec_out = dec_b[3 * unit : 4 * unit]
+    shard_cross_q = dec_b[4 * unit : 5 * unit]
+    shard_cross_kv = from_rows(dec_b[5 * unit : 7 * unit], 2)
+    shard_cross_out = dec_b[7 * unit :]
+    shard_enc_up = from_rows(enc_a[: 4 * unit], 4)
+    shard_enc_down = enc_a[4 * unit :]
+    shard_enc_qkv = from_rows(enc_b[: 3 * unit], 3)
+    shard_enc_out = enc_b[3 * unit : 4 * unit]
+    rest = enc_b[4 * unit :]
+    shard_enc_vecs = rest[:, :8]
+    shard_dec_vecs = rest[:, 8:21]
+    shard_lang = rest[:, 21:29]
+    shard_enc_bias_up = rest[:, 29:33].reshape(-1)
+    shard_dec_bias_up = rest[:, 33:37].reshape(-1)
     return (
         jnp.concatenate(dec_outputs, axis=0),
         jnp.concatenate(source_grads, axis=0),
@@ -585,7 +764,7 @@
 
 def solution(mesh):
     return jax.shard_map(
-        shards,
+        functools.partial(shards, Grid(mesh)),
         mesh=mesh,
         in_specs=(
             P(("dp", "fsdp"), None),

time: 2740 us -> 1120 us (0.41)
  waiting for transfers between devices: 1740 us -> 88.5 us
  blocking collectives: 567 us -> 0 us
  Pallas kernels: 0 us -> 465 us
  local copies, waits for them, and re-layouts: 94 us -> 163 us
  starting transfers between devices: 1.64 us -> 57 us
  other arithmetic: 58.8 us -> 100 us
    reduce_scatter x10 -> x0, waiting for transfers between devices: 1380 us -> none  [the longest x1 150 us: shards(): lax.psum_scatter(grad_enc_up, ('dp', 'fsdp'), scatter_dimension=0, tiled=...]
    all_gather x7 -> x0, blocking collectives: 486 us -> none  [the longest x1 74.5 us: shards(): lax.all_gather(cross_out, ('dp', 'fsdp'), axis=0, tiled=True)]
    pallas_call x0 -> x4, Pallas kernels: none -> 465 us  [place_weights(): pl.pallas_call(functools.partial(place_kernel, order, grid.nf, forms), ou...]
    unnamed x25 -> x0, waiting for transfers between devices: 364 us -> none
    ppermute x0 -> x48, waiting for transfers between devices: none -> 88.5 us  [the longest x24 73.5 us: swap_dp(): return lax.ppermute(value, 'dp', [(i, i ^ flip) for i in range(self.nd)])]
    unnamed x2 -> x0, blocking collectives: 80.5 us -> none
    ppermute x0 -> x48, starting transfers between devices: none -> 57 us  [the longest x24 38.3 us: swap_fsdp(): return lax.ppermute(value, 'fsdp', [(i, i ^ flip) for i in range(self.nf)])]
    gather x0 -> x8, local copies, waits for them, and re-layouts: none -> 28.5 us  [spread_grads(): sides.append(jnp.take(whole, jnp.array(table, jnp.int32) ^ me, axis=0))]
  transfers between devices with their start and end apart: 21 -> 48, of which waited for: 13 -> 11; matrix products, arithmetic and copies ran while one was open for 8% -> 14% of each run, Pallas kernels for 0% -> 29%
where the time goes in v1:
time: 1120 us; the launch traced here: 1110 us
  Pallas kernels  465 us (42%)
  matrix products  235 us (21%)
  local copies, waits for them, and re-layouts  163 us (15%)
  other arithmetic  100 us (9%)
  waiting for transfers between devices  88.5 us (8%)
  starting transfers between devices  57 us (5%)
    pallas_call x4, Pallas kernels, place_weights(): pl.pallas_call(functools.partial(place_kernel, order, grid.nf, forms), ou...  465 us
    ppermute x24, waiting for transfers between devices, swap_dp(): return lax.ppermute(value, 'dp', [(i, i ^ flip) for i in range(self.nd)])  73.5 us
    dot_general x22, matrix products, rows_inner(): lax.dot_general(left_operand, right_operand, (((0,), (0,)), ((), ())), pr...  62.8 us
    dot_general x24, matrix products, right_inner(): lax.dot_general(left_operand, right_operand, (((1,), (1,)), ((), ())), pr...  59.5 us
    unnamed x623, local copies, waits for them, and re-layouts  42.2 us
    ppermute x24, starting transfers between devices, swap_fsdp(): return lax.ppermute(value, 'fsdp', [(i, i ^ flip) for i in range(self.nf)])  38.3 us
    dot_general x22, matrix products, low_dot(): jnp.dot(left_operand, right_operand, preferred_element_type=jnp.float32)  31 us
    gather x8, local copies, waits for them, and re-layouts, spread_grads(): sides.append(jnp.take(whole, jnp.array(table, jnp.int32) ^ me, axis=0))  28.5 us
  transfers between devices with their start and end apart: 48, of which 11 were waited for; matrix products, arithmetic and copies ran while one was open for 14% of the time, Pallas kernels for 29%

profile of v1, /device:TPU:0, one launch (start us, length us, event | category | flops | bytes accessed | tf_op | source)
XLA Modules:
  0.0 1113.1 jit_solution(11864934387445933614)
XLA Ops:
  5.5 4.1 collective-permute-start.1
  18.0 3.8 collective-permute-start.8
  79.7 24.7 %collective-permute-done.15 = bf16[1,4,144,512]{3,2,1,0:T(8,128)(2,1)S(1)} collective-permute-done((bf16[1,4,144,512]{3,2,1,0:T(8,128)(2,1)S(1)}, bf16[1,4,144,512]{3,2,1,0:T(8,128)(2,1)S(1)}, u32[]{:S(2)}, u32[]{:S(2)}) %collective-permute-start.15) | collective-permute-done | bytes 589856 | tf_op jit(solution)/shard_map/ppermute | solution.py:417
  112.6 64.6 %shard_map.429 = (bf16[3,32,16,512]{3,2,1,0:T(8,128)(2,1)}, bf16[1,32,16,512]{3,2,1,0:T(8,128)(2,1)}) custom-call(s32[1]{0:T(128)} %bitcast.2.me_ref, bf16[16,4,16,512]{3,2,1,0:T(8,128)(2,1)} %bitcast.557, bf16[16,4,16,512]{3,2,1,0:T(8,128)(2,1)} %bitcast.623), custom_call_target="tpu_custom_call" | custom-call | tf_op jit(solution)/shard_map/pallas_call | solution.py:508
  210.0 128.2 %shard_map.430 = (bf16[3,32,16,512]{3,2,1,0:T(8,128)(2,1)}, bf16[1,32,16,512]{3,2,1,0:T(8,128)(2,1)}, bf16[1,32,16,512]{3,2,1,0:T(8,128)(2,1)}, bf16[2,32,16,512]{3,2,1,0:T(8,128)(2,1)}, bf16[1,32,16,512]{3,2,1,0:T(8,128)(2,1)}) custom-call(s32[1]{0:T(128)} %bitcast.2.me_ref, bf16[16,8,16,512]{3,2,1,0:T(8,128)(2,1)} %bitcast.23.mine, ...), custom_call_target="tpu_custom_call" | custom-call | tf_op jit(solution)/shard_map/pallas_call | solution.py:508
  362.2 128.2 %shard_map.432 = (bf16[4,32,16,512]{3,2,1,0:T(8,128)(2,1)}, bf16[32,4,16,512]{3,2,1,0:T(8,128)(2,1)}) custom-call(s32[1]{0:T(128)} %bitcast.2.me_ref, bf16[16,8,16,512]{3,2,1,0:T(8,128)(2,1)} %bitcast.87.mine, bf16[16,8,16,512]{3,2,1,0:T(8,128)(2,1)} %bitcast.89.other), custom_call_target="tpu_custom_call" | custom-call | tf_op jit(solution)/shard_map/pallas_call | solution.py:508
  503.1 144.1 %shard_map.431 = (bf16[1,32,16,512]{3,2,1,0:T(8,128)(2,1)}, bf16[4,32,16,512]{3,2,1,0:T(8,128)(2,1)}, bf16[32,4,16,512]{3,2,1,0:T(8,128)(2,1)}) custom-call(s32[1]{0:T(128)} %bitcast.2.me_ref, bf16[16,9,16,512]{3,2,1,0:T(8,128)(2,1)} %bitcast.57.mine, bf16[16,9,16,512]{3,2,1,0:T(8,128)(2,1)} %bitcast.59.other), custom_call_target="tpu_custom_call" | custom-call | tf_op jit(solution)/shard_map/pallas_call | solution.py:508
  698.5 4.0 fusion.248
  702.5 10.7 convert_reduce_fusion.1
  713.2 5.6 multiply_reduce_fusion.8
  775.8 4.5 convert_reduce_fusion.3
  780.3 4.3 fusion.213
  785.1 4.6 convert_reduce_fusion.2
  801.7 3.7 add_convert_fusion
  808.1 4.7 reshape.1046
  817.7 4.4 gather_fusion.7
  822.1 4.3 gather_fusion.6
  826.4 7.4 add_convert_fusion.2
  836.5 4.5 reshape.1030
  845.8 4.4 gather_fusion.3
  850.2 4.3 gather_fusion.2
  858.0 5.8 convert_reduce_fusion.22
  863.8 5.4 multiply_reduce_fusion.2
  972.1 4.3 gather_fusion.4
  980.8 4.7 broadcast_select_fusion.1
  1000.7 10.1 collective-permute-done.25
  1013.7 4.0 convert_add_fusion
  1036.7 9.8 collective-permute-done.31
  1049.3 17.3 %collective-permute-done.43 = bf16[2,4,128,512]{3,2,1,0:T(8,128)(2,1)S(1)} collective-permute-done((bf16[2,4,128,512]{3,2,1,0:T(8,128)(2,1)}, bf16[2,4,128,512]{3,2,1,0:T(8,128)(2,1)S(1)}, u32[]{:S(2)}, u32[]{:S(2)}) %collective-permute-start.43) | collective-permute-done | bytes 1048608 | tf_op jit(solution)/shard_map/ppermute | solution.py:417
  1072.3 8.6 collective-permute-done.38
  1090.2 4.9 collective-permute-start.45
  1098.7 7.1 collective-permute-done.34
  (1055 shorter events, 457.0 us)
Async XLA Ops:
  5.5 25.8 %collective-permute-start.1 = (bf16[64,512]{1,0:T(8,128)(2,1)S(1)}, bf16[64,512]{1,0:T(8,128)(2,1)}, u32[]{:S(2)}, u32[]{:S(2)}) collective-permute-start(bf16[64,512]{1,0:T(8,128)(2,1)S(1)} %get-tuple-element.258), channel_id=1, source_target_pairs={{0,2},{1,3},{2,0},{3,1},{4,6},{5,7},{6,4},{7,5},{8,10},{9,11},{10,... | collective-permute-start | bytes 196616 | tf_op jit(solution)/shard_map/ppermute | solution.py:420
  9.6 22.4 %collective-permute-start = (bf16[64,512]{1,0:T(8,128)(2,1)S(1)}, bf16[64,512]{1,0:T(8,128)(2,1)}, u32[]{:S(2)}, u32[]{:S(2)}) collective-permute-start(bf16[64,512]{1,0:T(8,128)(2,1)S(1)} %get-tuple-element.258), channel_id=1, source_target_pairs={{0,1},{1,0},{2,3},{3,2},{4,5},{5,4},{6,7},{7,6},{8,9},{9,8},{10,11... | collective-permute-start | bytes 196616 | tf_op jit(solution)/shard_map/ppermute | solution.py:420
  11.2 23.2 %collective-permute-start.2 = (bf16[64,512]{1,0:T(8,128)(2,1)S(1)}, bf16[64,512]{1,0:T(8,128)(2,1)}, u32[]{:S(2)}, u32[]{:S(2)}) collective-permute-start(bf16[64,512]{1,0:T(8,128)(2,1)S(1)} %get-tuple-element.258), channel_id=1, source_target_pairs={{0,3},{1,2},{2,1},{3,0},{4,7},{5,6},{6,5},{7,4},{8,11},{9,10},{10,... | collective-permute-start | bytes 196616 | tf_op jit(solution)/shard_map/ppermute | solution.py:420
  18.0 19.3 %collective-permute-start.8 = (bf16[128,512]{1,0:T(8,128)(2,1)}, bf16[128,512]{1,0:T(8,128)(2,1)}, u32[]{:S(2)}, u32[]{:S(2)}) collective-permute-start(bf16[128,512]{1,0:T(8,128)(2,1)} %constant_dynamic-update-slice_fusion), channel_id=1, source_target_pairs={{0,3},{1,2},{2,1},{3,0},{4,7},{5,6},{6,5},{7,4},{8,11},{9,10},{10,... | collective-permute-start | bytes 393224 | tf_op jit(solution)/shard_map/ppermute | solution.py:420
  21.9 15.6 %collective-permute-start.7 = (bf16[128,512]{1,0:T(8,128)(2,1)}, bf16[128,512]{1,0:T(8,128)(2,1)}, u32[]{:S(2)}, u32[]{:S(2)}) collective-permute-start(bf16[128,512]{1,0:T(8,128)(2,1)} %constant_dynamic-update-slice_fusion), channel_id=1, source_target_pairs={{0,2},{1,3},{2,0},{3,1},{4,6},{5,7},{6,4},{7,5},{8,10},{9,11},{10,... | collective-permute-start | bytes 393224 | tf_op jit(solution)/shard_map/ppermute | solution.py:420
  40.2 14.3 %collective-permute-start.9 = (bf16[1,4,128,512]{3,2,1,0:T(8,128)(2,1)S(1)}, bf16[1,4,128,512]{3,2,1,0:T(8,128)(2,1)S(1)}, u32[]{:S(2)}, u32[]{:S(2)}) collective-permute-start(bf16[1,4,128,512]{3,2,1,0:T(8,128)(2,1)S(1)} %maximum_bitcast_fusion.1), channel_id=1, source_target_pairs={{0,8},{4,12},{8,0},{12,4},{16,24},{20,28},{24,16},{28,20},{1,9},{5... | collective-permute-start | bytes 1572872 | tf_op jit(solution)/shard_map/ppermute | solution.py:417
  44.5 24.3 %collective-permute-start.13 = (bf16[144,512]{1,0:T(8,128)(2,1)}, bf16[144,512]{1,0:T(8,128)(2,1)}, u32[]{:S(2)}, u32[]{:S(2)}) collective-permute-start(bf16[144,512]{1,0:T(8,128)(2,1)} %get-tuple-element.254), channel_id=1, source_target_pairs={{0,2},{1,3},{2,0},{3,1},{4,6},{5,7},{6,4},{7,5},{8,10},{9,11},{10,... | collective-permute-start | bytes 442376 | tf_op jit(solution)/shard_map/ppermute | solution.py:420
  46.5 23.9 %collective-permute-start.12 = (bf16[144,512]{1,0:T(8,128)(2,1)}, bf16[144,512]{1,0:T(8,128)(2,1)}, u32[]{:S(2)}, u32[]{:S(2)}) collective-permute-start(bf16[144,512]{1,0:T(8,128)(2,1)} %get-tuple-element.254), channel_id=1, source_target_pairs={{0,1},{1,0},{2,3},{3,2},{4,5},{5,4},{6,7},{7,6},{8,9},{9,8},{10,11... | collective-permute-start | bytes 442376 | tf_op jit(solution)/shard_map/ppermute | solution.py:420
  48.0 23.7 %collective-permute-start.21 = (bf16[1,4,128,512]{3,2,1,0:T(8,128)(2,1)S(1)}, bf16[1,4,128,512]{3,2,1,0:T(8,128)(2,1)}, u32[]{:S(2)}, u32[]{:S(2)}) collective-permute-start(bf16[1,4,128,512]{3,2,1,0:T(8,128)(2,1)S(1)} %maximum_bitcast_fusion.2), channel_id=1, source_target_pairs={{0,16},{4,20},{8,24},{12,28},{16,0},{20,4},{24,8},{28,12},{1,17},{... | collective-permute-start | bytes 1572872 | tf_op jit(solution)/shard_map/ppermute | solution.py:417
  50.5 24.5 %collective-permute-start.4 = (bf16[2,4,64,512]{3,2,1,0:T(8,128)(2,1)}, bf16[2,4,64,512]{3,2,1,0:T(8,128)(2,1)}, u32[]{:S(2)}, u32[]{:S(2)}) collective-permute-start(bf16[2,4,64,512]{3,2,1,0:T(8,128)(2,1)} %pad_maximum_fusion.36), channel_id=1, source_target_pairs={{0,16},{4,20},{8,24},{12,28},{16,0},{20,4},{24,8},{28,12},{1,17},{... | collective-permute-start | bytes 1572872 | tf_op jit(solution)/shard_map/ppermute | solution.py:417
  55.4 15.1 %collective-permute-start.14 = (bf16[144,512]{1,0:T(8,128)(2,1)}, bf16[144,512]{1,0:T(8,128)(2,1)}, u32[]{:S(2)}, u32[]{:S(2)}) collective-permute-start(bf16[144,512]{1,0:T(8,128)(2,1)} %get-tuple-element.254), channel_id=1, source_target_pairs={{0,3},{1,2},{2,1},{3,0},{4,7},{5,6},{6,5},{7,4},{8,11},{9,10},{10,... | collective-permute-start | bytes 442376 | tf_op jit(solution)/shard_map/ppermute | solution.py:420
  68.9 38.2 %collective-permute-start.10 = (bf16[2,4,128,512]{3,2,1,0:T(8,128)(2,1)S(1)}, bf16[2,4,128,512]{3,2,1,0:T(8,128)(2,1)S(1)}, u32[]{:S(2)}, u32[]{:S(2)}) collective-permute-start(bf16[2,4,128,512]{3,2,1,0:T(8,128)(2,1)S(1)} %pad_maximum_fusion.16), channel_id=1, source_target_pairs={{0,16},{4,20},{8,24},{12,28},{16,0},{20,4},{24,8},{28,12},{1,17},{... | collective-permute-start | bytes 3145736 | tf_op jit(solution)/shard_map/ppermute | solution.py:417
  72.9 35.7 %collective-permute-start.22 = (bf16[2,4,128,512]{3,2,1,0:T(8,128)(2,1)S(1)}, bf16[2,4,128,512]{3,2,1,0:T(8,128)(2,1)S(1)}, u32[]{:S(2)}, u32[]{:S(2)}) collective-permute-start(bf16[2,4,128,512]{3,2,1,0:T(8,128)(2,1)S(1)} %pad_maximum_fusion.18), channel_id=1, source_target_pairs={{0,8},{4,12},{8,0},{12,4},{16,24},{20,28},{24,16},{28,20},{1,9},{5... | collective-permute-start | bytes 3145736 | tf_op jit(solution)/shard_map/ppermute | solution.py:417
  74.4 30.0 %collective-permute-start.15 = (bf16[1,4,144,512]{3,2,1,0:T(8,128)(2,1)S(1)}, bf16[1,4,144,512]{3,2,1,0:T(8,128)(2,1)S(1)}, u32[]{:S(2)}, u32[]{:S(2)}) collective-permute-start(bf16[1,4,144,512]{3,2,1,0:T(8,128)(2,1)S(1)} %maximum_bitcast_fusion), channel_id=1, source_target_pairs={{0,16},{4,20},{8,24},{12,28},{16,0},{20,4},{24,8},{28,12},{1,17},{... | collective-permute-start | bytes 1769480 | tf_op jit(solution)/shard_map/ppermute | solution.py:417
  76.2 35.5 %collective-permute-start.5 = (bf16[16,64,512]{2,1,0:T(8,128)(2,1)S(1)}, bf16[16,64,512]{2,1,0:T(8,128)(2,1)S(1)}, u32[]{:S(2)}, u32[]{:S(2)}) collective-permute-start(bf16[16,64,512]{2,1,0:T(8,128)(2,1)S(1)} %bitcast.556), channel_id=1, source_target_pairs={{0,4},{4,0},{8,12},{12,8},{16,20},{20,16},{24,28},{28,24},{1,5},{5... | collective-permute-start | bytes 3145736 | tf_op jit(solution)/shard_map/ppermute | solution.py:417
  105.6 101.5 %collective-permute-start.16 = (bf16[2,4,144,512]{3,2,1,0:T(8,128)(2,1)}, bf16[2,4,144,512]{3,2,1,0:T(8,128)(2,1)}, u32[]{:S(2)}, u32[]{:S(2)}) collective-permute-start(bf16[2,4,144,512]{3,2,1,0:T(8,128)(2,1)} %pad_maximum_fusion.14), channel_id=1, source_target_pairs={{0,8},{4,12},{8,0},{12,4},{16,24},{20,28},{24,16},{28,20},{1,9},{5... | collective-permute-start | bytes 3538952 | tf_op jit(solution)/shard_map/ppermute | solution.py:417
  108.6 101.4 %collective-permute-start.11 = (bf16[16,128,512]{2,1,0:T(8,128)(2,1)}, bf16[16,128,512]{2,1,0:T(8,128)(2,1)}, u32[]{:S(2)}, u32[]{:S(2)}) collective-permute-start(bf16[16,128,512]{2,1,0:T(8,128)(2,1)} %bitcast.24), channel_id=1, source_target_pairs={{0,4},{4,0},{8,12},{12,8},{16,20},{20,16},{24,28},{28,24},{1,5},{5... | collective-permute-start | bytes 6291464 | tf_op jit(solution)/shard_map/ppermute | solution.py:417
  111.2 251.0 %collective-permute-start.23 = (bf16[16,128,512]{2,1,0:T(8,128)(2,1)}, bf16[16,128,512]{2,1,0:T(8,128)(2,1)}, u32[]{:S(2)}, u32[]{:S(2)}) collective-permute-start(bf16[16,128,512]{2,1,0:T(8,128)(2,1)} %bitcast.88), channel_id=1, source_target_pairs={{0,4},{4,0},{8,12},{12,8},{16,20},{20,16},{24,28},{28,24},{1,5},{5... | collective-permute-start | bytes 6291464 | tf_op jit(solution)/shard_map/ppermute | solution.py:417
  210.0 293.1 %collective-permute-start.17 = (bf16[16,144,512]{2,1,0:T(8,128)(2,1)}, bf16[16,144,512]{2,1,0:T(8,128)(2,1)}, u32[]{:S(2)}, u32[]{:S(2)}) collective-permute-start(bf16[16,144,512]{2,1,0:T(8,128)(2,1)} %bitcast.58), channel_id=1, source_target_pairs={{0,4},{4,0},{8,12},{12,8},{16,20},{20,16},{24,28},{28,24},{1,5},{5... | collective-permute-start | bytes 7077896 | tf_op jit(solution)/shard_map/ppermute | solution.py:417
  985.5 28.2 %collective-permute-start.42 = (bf16[16,128,512]{2,1,0:T(8,128)(2,1)}, bf16[16,128,512]{2,1,0:T(8,128)(2,1)}, u32[]{:S(2)}, u32[]{:S(2)}) collective-permute-start(bf16[16,128,512]{2,1,0:T(8,128)(2,1)} %get-tuple-element.312), channel_id=1, source_target_pairs={{0,4},{4,0},{8,12},{12,8},{16,20},{20,16},{24,28},{28,24},{1,5},{5... | collective-permute-start | bytes 6291464 | tf_op jit(solution)/shard_map/ppermute | solution.py:417
  985.6 28.1 %collective-permute-start.30 = (bf16[16,128,512]{2,1,0:T(8,128)(2,1)}, bf16[16,128,512]{2,1,0:T(8,128)(2,1)}, u32[]{:S(2)}, u32[]{:S(2)}) collective-permute-start(bf16[16,128,512]{2,1,0:T(8,128)(2,1)} %get-tuple-element.313), channel_id=1, source_target_pairs={{0,4},{4,0},{8,12},{12,8},{16,20},{20,16},{24,28},{28,24},{1,5},{5... | collective-permute-start | bytes 6291464 | tf_op jit(solution)/shard_map/ppermute | solution.py:417
  987.7 36.5 %collective-permute-start.36 = (bf16[16,128,512]{2,1,0:T(8,128)(2,1)}, bf16[16,128,512]{2,1,0:T(8,128)(2,1)}, u32[]{:S(2)}, u32[]{:S(2)}) collective-permute-start(bf16[16,128,512]{2,1,0:T(8,128)(2,1)} %broadcast_select_fusion), channel_id=1, source_target_pairs={{0,4},{4,0},{8,12},{12,8},{16,20},{20,16},{24,28},{28,24},{1,5},{5... | collective-permute-start | bytes 6291464 | tf_op jit(solution)/shard_map/ppermute | solution.py:417
  993.8 16.9 %collective-permute-start.25 = (bf16[2,4,80,512]{3,2,1,0:T(8,128)(2,1)}, bf16[2,4,80,512]{3,2,1,0:T(8,128)(2,1)}, u32[]{:S(2)}, u32[]{:S(2)}) collective-permute-start(bf16[2,4,80,512]{3,2,1,0:T(8,128)(2,1)} %bitcast.200), channel_id=1, source_target_pairs={{0,8},{4,12},{8,0},{12,4},{16,24},{20,28},{24,16},{28,20},{1,9},{5... | collective-permute-start | bytes 1966088 | tf_op jit(solution)/shard_map/ppermute | solution.py:417
  1020.1 26.4 %collective-permute-start.31 = (bf16[2,4,128,512]{3,2,1,0:T(8,128)(2,1)}, bf16[2,4,128,512]{3,2,1,0:T(8,128)(2,1)}, u32[]{:S(2)}, u32[]{:S(2)}) collective-permute-start(bf16[2,4,128,512]{3,2,1,0:T(8,128)(2,1)} %bitcast.213), channel_id=1, source_target_pairs={{0,16},{4,20},{8,24},{12,28},{16,0},{20,4},{24,8},{28,12},{1,17},{... | collective-permute-start | bytes 3145736 | tf_op jit(solution)/shard_map/ppermute | solution.py:417
  1020.6 46.1 %collective-permute-start.43 = (bf16[2,4,128,512]{3,2,1,0:T(8,128)(2,1)}, bf16[2,4,128,512]{3,2,1,0:T(8,128)(2,1)S(1)}, u32[]{:S(2)}, u32[]{:S(2)}) collective-permute-start(bf16[2,4,128,512]{3,2,1,0:T(8,128)(2,1)} %bitcast.254), channel_id=1, source_target_pairs={{0,16},{4,20},{8,24},{12,28},{16,0},{20,4},{24,8},{28,12},{1,17},{... | collective-permute-start | bytes 3145736 | tf_op jit(solution)/shard_map/ppermute | solution.py:417
  1031.5 36.2 %collective-permute-start.37 = (bf16[2,4,128,512]{3,2,1,0:T(8,128)(2,1)}, bf16[2,4,128,512]{3,2,1,0:T(8,128)(2,1)}, u32[]{:S(2)}, u32[]{:S(2)}) collective-permute-start(bf16[2,4,128,512]{3,2,1,0:T(8,128)(2,1)} %bitcast.239), channel_id=1, source_target_pairs={{0,8},{4,12},{8,0},{12,4},{16,24},{20,28},{24,16},{28,20},{1,9},{5... | collective-permute-start | bytes 3145736 | tf_op jit(solution)/shard_map/ppermute | solution.py:417
  1048.7 21.4 %collective-permute-start.32 = (bf16[1,4,128,512]{3,2,1,0:T(8,128)(2,1)S(1)}, bf16[1,4,128,512]{3,2,1,0:T(8,128)(2,1)S(1)}, u32[]{:S(2)}, u32[]{:S(2)}) collective-permute-start(bf16[1,4,128,512]{3,2,1,0:T(8,128)(2,1)S(1)} %slice.714), channel_id=1, source_target_pairs={{0,8},{4,12},{8,0},{12,4},{16,24},{20,28},{24,16},{28,20},{1,9},{5... | collective-permute-start | bytes 1572872 | tf_op jit(solution)/shard_map/ppermute | solution.py:417
  1067.1 16.1 %collective-permute-start.44 = (bf16[1,4,128,512]{3,2,1,0:T(8,128)(2,1)S(1)}, bf16[1,4,128,512]{3,2,1,0:T(8,128)(2,1)S(1)}, u32[]{:S(2)}, u32[]{:S(2)}) collective-permute-start(bf16[1,4,128,512]{3,2,1,0:T(8,128)(2,1)S(1)} %slice.712), channel_id=1, source_target_pairs={{0,8},{4,12},{8,0},{12,4},{16,24},{20,28},{24,16},{28,20},{1,9},{5... | collective-permute-start | bytes 1572872 | tf_op jit(solution)/shard_map/ppermute | solution.py:417
  1070.4 28.2 %collective-permute-start.33 = (bf16[128,512]{1,0:T(8,128)(2,1)S(1)}, bf16[128,512]{1,0:T(8,128)(2,1)S(1)}, u32[]{:S(2)}, u32[]{:S(2)}) collective-permute-start(bf16[128,512]{1,0:T(8,128)(2,1)S(1)} %get-tuple-element.234), channel_id=1, source_target_pairs={{0,1},{1,0},{2,3},{3,2},{4,5},{5,4},{6,7},{7,6},{8,9},{9,8},{10,11... | collective-permute-start | bytes 393224 | tf_op jit(solution)/shard_map/ppermute | solution.py:420
  1070.8 27.9 %collective-permute-start.35 = (bf16[128,512]{1,0:T(8,128)(2,1)S(1)}, bf16[128,512]{1,0:T(8,128)(2,1)S(1)}, u32[]{:S(2)}, u32[]{:S(2)}) collective-permute-start(bf16[128,512]{1,0:T(8,128)(2,1)S(1)} %get-tuple-element.235), channel_id=1, source_target_pairs={{0,3},{1,2},{2,1},{3,0},{4,7},{5,6},{6,5},{7,4},{8,11},{9,10},{10,... | collective-permute-start | bytes 393224 | tf_op jit(solution)/shard_map/ppermute | solution.py:420
  1086.4 19.4 %collective-permute-start.34 = (bf16[128,512]{1,0:T(8,128)(2,1)S(1)}, bf16[128,512]{1,0:T(8,128)(2,1)S(1)}, u32[]{:S(2)}, u32[]{:S(2)}) collective-permute-start(bf16[128,512]{1,0:T(8,128)(2,1)S(1)} %get-tuple-element.236), channel_id=1, source_target_pairs={{0,2},{1,3},{2,0},{3,1},{4,6},{5,7},{6,4},{7,5},{8,10},{9,11},{10,... | collective-permute-start | bytes 393224 | tf_op jit(solution)/shard_map/ppermute | solution.py:420
  1090.2 17.6 %collective-permute-start.45 = (bf16[128,512]{1,0:T(8,128)(2,1)S(1)}, bf16[128,512]{1,0:T(8,128)(2,1)S(1)}, u32[]{:S(2)}, u32[]{:S(2)}) collective-permute-start(bf16[128,512]{1,0:T(8,128)(2,1)S(1)} %get-tuple-element.228), channel_id=1, source_target_pairs={{0,1},{1,0},{2,3},{3,2},{4,5},{5,4},{6,7},{7,6},{8,9},{9,8},{10,11... | collective-permute-start | bytes 393224 | tf_op jit(solution)/shard_map/ppermute | solution.py:420
  (317 other events, 4061.3 us)
